TPU v7x, 32 devices: a whole 2x2x4 slice. The times are simulated.
32 devices in a mesh: seg: 8 (over y, x, core), blk: 4 (over z).
Axes of the slice: x: 2, y: 2, z: 4, core: 2. Of those that a mesh axis runs over, the one named last changes fastest.
Arguments:
- spectra: bfloat16 [8, 4, 128, 4096], P('seg', 'blk'), may hold values from -6 to 6
- source_channels: int32 [4, 64], P('blk'), may hold values from 0 to 127, as said below
- pair_mask: int32 [4, 4], P('blk'), may hold values from 0 to 1, as said below
- channel_counts: int32 [4], P('blk'), may hold values from 64 to 128, as said below
Outputs:
- stacked: float32 [4, 4, 128, 1024], P('blk', None, 'seg')
Inputs may be any that keep to these rules, and one draw needn't show every extreme that they name: `channel_counts`: every block has at least 64 live channels, and some block has all 128. `source_channels`: each block's 64 sources are distinct live channels of that block. `pair_mask`: slots whose offset leads past the fibre's ends are 0.
All inputs are finite; a program needn't handle non-finite values.
Results may differ from a plain program's by a relative error of at most 0.0095.
Values may be sent and summed in bfloat16 or wider, within the bound.
A program may use at most 64 MiB of HBM per device.

v0:
```python
import math

import jax
import jax.numpy as jnp
from jax import lax
from jax.sharding import PartitionSpec as P

LAGS = 16
REACH = 2


def passed_along(value, axis, by):
    devices = lax.axis_size(axis)
    pairs = [(i, i + by) for i in range(devices) if 0 <= i + by < devices]
    return lax.ppermute(value, axis, pairs)


def slot_offsets():
    return [
        slot_index - REACH if slot_index < REACH else slot_index - REACH + 1
        for slot_index in range(2 * REACH)
    ]


def make_table(bin_count, lag_count):
    freq_index = lax.broadcasted_iota(jnp.int32, (bin_count, lag_count), 0)
    lag_index = lax.broadcasted_iota(jnp.int32, (bin_count, lag_count), 1) - lag_count // 2
    turn_count = jnp.mod(freq_index * lag_index, 2 * bin_count)
    phase_angle = turn_count.astype(jnp.float32) * (math.pi / bin_count)
    scaling = 1.0 / math.sqrt(2.0 * bin_count)
    return jnp.concatenate(
        [jnp.cos(phase_angle) * scaling, -jnp.sin(phase_angle) * scaling], axis=0
    ).astype(jnp.bfloat16)


def source_kernel(sources, table):
    bin_count = table.shape[0] // 2
    source_re = sources[:, :bin_count].astype(jnp.float32).T[:, :, None]
    source_im = sources[:, bin_count:].astype(jnp.float32).T[:, :, None]
    table_re = table[:bin_count].astype(jnp.float32)[:, None, :]
    table_im = table[bin_count:].astype(jnp.float32)[:, None, :]
    upper = source_re * table_re + source_im * table_im
    lower = source_im * table_re - source_re * table_im
    joined = jnp.concatenate([upper, lower], axis=0)
    return joined.reshape(2 * bin_count, -1).astype(jnp.bfloat16)


def local(spectra, source_channels, pair_mask, channel_counts):
    own_block = spectra[0, 0]
    channels = own_block.shape[0]
    bin_count = own_block.shape[1] // 2
    lag_table = make_table(bin_count, LAGS)
    live_rows = lax.broadcasted_iota(jnp.int32, (channels, 1), 0) < channel_counts[0]
    own_block = jnp.where(live_rows, own_block, jnp.zeros_like(own_block))
    sources = jnp.take(own_block, source_channels[0], axis=0)
    weights = pair_mask[0].astype(jnp.float32)
    offsets = slot_offsets()
    term_list = []
    kernel = source_kernel(sources, lag_table)
    for slot_index, offset in enumerate(offsets):
        nearby = passed_along(own_block, "blk", -offset)
        term_list.append(
            jnp.dot(nearby, kernel, preferred_element_type=jnp.float32) * weights[slot_index]
        )
    reduced = lax.psum_scatter(jnp.stack(term_list), "seg", scatter_dimension=1, tiled=True)
    stacked = reduced * (1.0 / math.sqrt(lax.axis_size("seg")))
    return stacked[None]


def solution(mesh):
    in_specs = (P("seg", "blk", None, None), P("blk", None), P("blk", None), P("blk"))
    out_specs = P("blk", None, "seg", None)
    return jax.shard_map(local, mesh=mesh, in_specs=in_specs, out_specs=out_specs, check_vma=False)
```

profile of v0, /device:TPU:0, one launch (start us, length us, event | category | flops | bytes accessed | tf_op | source)
XLA Modules:
  0.0 147.9 jit_solution(10115173024602982549)
XLA Ops:
  6.5 0.0 reduce-scatter.2.cloned.1.call-start
  7.2 1.4 bitcast_select_fusion
  8.6 0.0 copy-start
  8.6 6.9 %collective-permute-start = (bf16[128,4096]{1,0:T(8,128)(2,1)S(1)}, bf16[128,4096]{1,0:T(8,128)(2,1)}, u32[]{:S(2)}, u32[]{:S(2)}) collective-permute-start(bf16[128,4096]{1,0:T(8,128)(2,1)S(1)} %bitcast_select_fusion), channel_id=1, source_target_pairs={{0,2},{1,3},{4,6},{5,7},{8,10},{9,11},{12,14},{13,15},{16,18},{17,... | collective-permute-start | bytes 3145736 | tf_op jit(solution)/shard_map/ppermute | solution.py:15
  15.5 4.5 %collective-permute-start.1 = (bf16[128,4096]{1,0:T(8,128)(2,1)S(1)}, bf16[128,4096]{1,0:T(8,128)(2,1)}, u32[]{:S(2)}, u32[]{:S(2)}) collective-permute-start(bf16[128,4096]{1,0:T(8,128)(2,1)S(1)} %bitcast_select_fusion), channel_id=1, source_target_pairs={{0,1},{1,2},{2,3},{4,5},{5,6},{6,7},{8,9},{9,10},{10,11},{12,13},{... | collective-permute-start | bytes 3145736 | tf_op jit(solution)/shard_map/ppermute | solution.py:15
  20.0 1.3 collective-permute-start.2
  21.3 1.3 collective-permute-start.3
  22.6 0.7 fusion.12
  23.3 0.7 compare_and_fusion
  23.9 0.9 gather_fusion
  24.8 0.1 broadcast_select_fusion
  24.9 0.1 convert_bitcast_fusion.1
  25.0 0.0 copy-done
  25.1 0.7 fusion.13
  25.7 0.6 fusion.10
  26.3 2.9 %add_convert_fusion = (bf16[2048,64,16]{0,2,1:T(8,128)(2,1)S(1)}, bf16[2048,64,16]{0,2,1:T(8,128)(2,1)S(1)}) fusion(f32[2048,16]{0,1:T(8,128)S(1)} %get-tuple-element.14, f32[2048,64]{0,1:T(8,128)S(1)} %get-tuple-element.8, f32[2048,16]{0,1:T(8,128)S(1)} %get-tuple-element.13, f32[2048,64]{0,1:T(8,128)S(1)} %get-tuple-element.7), kind=kLoop, calls=%fused_computation.3 | loop fusion | flops 16777216 | bytes 9699328 | tf_op jit(solution)/shard_map/convert.5
  29.2 8.9 %collective-permute-done = bf16[128,4096]{1,0:T(8,128)(2,1)} collective-permute-done((bf16[128,4096]{1,0:T(8,128)(2,1)S(1)}, bf16[128,4096]{1,0:T(8,128)(2,1)}, u32[]{:S(2)}, u32[]{:S(2)}) %collective-permute-start) | collective-permute-done | bytes 1048608 | tf_op jit(solution)/shard_map/ppermute | solution.py:15
  38.1 4.8 %fusion.3 = f32[1,128,1024]{2,1,0:T(8,128)S(1)} fusion(bf16[128,4096]{1,0:T(8,128)(2,1)} %collective-permute-done, f32[]{:T(128)} %bitcast.9, bf16[2048,1024]{0,1:T(8,128)(2,1)S(1)} %bitcast.38, bf16[2048,1024]{0,1:T(8,128)(2,1)S(1)} %bitcast.34), kind=kOutput, calls=%fused_computation.12 | convolution fusion | flops 1090650112 | bytes 9961476 | tf_op jit(solution)/shard_map/dot_general | solution.py:63
  42.9 16.6 %collective-permute-done.1 = bf16[128,4096]{1,0:T(8,128)(2,1)} collective-permute-done((bf16[128,4096]{1,0:T(8,128)(2,1)S(1)}, bf16[128,4096]{1,0:T(8,128)(2,1)}, u32[]{:S(2)}, u32[]{:S(2)}) %collective-permute-start.1) | collective-permute-done | bytes 1048608 | tf_op jit(solution)/shard_map/ppermute | solution.py:15
  59.4 4.8 %fusion.2 = f32[1,128,1024]{2,1,0:T(8,128)S(1)} fusion(bf16[128,4096]{1,0:T(8,128)(2,1)} %collective-permute-done.1, f32[]{:T(128)} %bitcast.11, bf16[2048,1024]{0,1:T(8,128)(2,1)S(1)} %bitcast.39, bf16[2048,1024]{0,1:T(8,128)(2,1)S(1)} %bitcast.35), kind=kOutput, calls=%fused_computation.10 | convolution fusion | flops 1090650112 | bytes 9961476 | tf_op jit(solution)/shard_map/dot_general | solution.py:63
  64.2 0.0 collective-permute-done.2
  64.2 4.7 %fusion.1 = f32[1,128,1024]{2,1,0:T(8,128)S(1)} fusion(bf16[128,4096]{1,0:T(8,128)(2,1)} %collective-permute-done.2, f32[]{:T(128)} %bitcast.13, bf16[2048,1024]{0,1:T(8,128)(2,1)S(1)} %bitcast.40, bf16[2048,1024]{0,1:T(8,128)(2,1)S(1)} %bitcast.36), kind=kOutput, calls=%fused_computation.8 | convolution fusion | flops 1090650112 | bytes 9961476 | tf_op jit(solution)/shard_map/dot_general | solution.py:63
  68.9 21.0 %collective-permute-done.3 = bf16[128,4096]{1,0:T(8,128)(2,1)S(1)} collective-permute-done((bf16[128,4096]{1,0:T(8,128)(2,1)S(1)}, bf16[128,4096]{1,0:T(8,128)(2,1)S(1)}, u32[]{:S(2)}, u32[]{:S(2)}) %collective-permute-start.3) | collective-permute-done | bytes 1048608 | tf_op jit(solution)/shard_map/ppermute | solution.py:15
  89.9 4.0 %fusion = f32[1,128,1024]{2,1,0:T(8,128)S(1)} fusion(bf16[128,4096]{1,0:T(8,128)(2,1)S(1)} %collective-permute-done.3, f32[]{:T(128)} %bitcast.15, bf16[2048,1024]{0,1:T(8,128)(2,1)S(1)} %bitcast.41, bf16[2048,1024]{0,1:T(8,128)(2,1)S(1)} %bitcast.37), kind=kOutput, calls=%fused_computation.6 | convolution fusion | flops 1090650112 | bytes 9961476 | tf_op jit(solution)/shard_map/dot_general | solution.py:63
  93.9 1.5 pad_maximum_fusion.1
  95.4 0.0 reduce-scatter.2.cloned.1.call-update
  95.4 44.0 %reduce-scatter.2.cloned.1.call-done = f32[4,16,1024]{2,1,0:T(8,128)} async-done(((f32[4,128,1024]{2,1,0:T(8,128)}), f32[4,16,1024]{2,1,0:T(8,128)}) %reduce-scatter.2.cloned.1.call-update) | async-done | bytes 262160 | tf_op jit(solution)/shard_map/reduce_scatter | solution.py:65
  139.4 1.7 %multiply_bitcast_fusion = f32[1,4,16,1024]{3,2,1,0:T(8,128)} fusion(f32[4,16,1024]{2,1,0:T(8,128)} %reduce-scatter.2.cloned.1.call-done), kind=kLoop, calls=%fused_computation.17 | loop fusion | flops 65536 | bytes 524288 | tf_op jit(solution)/shard_map/broadcast_in_dim | solution.py:67
  (4 shorter events, 0.0 us)
Async XLA Ops:
  6.5 132.9 %reduce-scatter.2.cloned.1.call-start = ((), (), s32[]{:S(2)}) async-start(), calls=%async_computation.1 | async-start | bytes 2359296 | tf_op jit(solution)/shard_map/reduce_scatter | solution.py:65
  8.6 16.5 %copy-start = (s32[1,4]{1,0:T(1,128)S(1)}, s32[1,4]{1,0:T(1,128)}, u32[]{:S(2)}) copy-start(s32[1,4]{1,0:T(1,128)} %param.6) | copy-start | bytes 52
  8.6 29.5 %collective-permute-start = (bf16[128,4096]{1,0:T(8,128)(2,1)S(1)}, bf16[128,4096]{1,0:T(8,128)(2,1)}, u32[]{:S(2)}, u32[]{:S(2)}) collective-permute-start(bf16[128,4096]{1,0:T(8,128)(2,1)S(1)} %bitcast_select_fusion), channel_id=1, source_target_pairs={{0,2},{1,3},{4,6},{5,7},{8,10},{9,11},{12,14},{13,15},{16,18},{17,... | collective-permute-start | bytes 3145736 | tf_op jit(solution)/shard_map/ppermute | solution.py:15
  15.5 43.9 %collective-permute-start.1 = (bf16[128,4096]{1,0:T(8,128)(2,1)S(1)}, bf16[128,4096]{1,0:T(8,128)(2,1)}, u32[]{:S(2)}, u32[]{:S(2)}) collective-permute-start(bf16[128,4096]{1,0:T(8,128)(2,1)S(1)} %bitcast_select_fusion), channel_id=1, source_target_pairs={{0,1},{1,2},{2,3},{4,5},{5,6},{6,7},{8,9},{9,10},{10,11},{12,13},{... | collective-permute-start | bytes 3145736 | tf_op jit(solution)/shard_map/ppermute | solution.py:15
  20.0 44.2 %collective-permute-start.2 = (bf16[128,4096]{1,0:T(8,128)(2,1)S(1)}, bf16[128,4096]{1,0:T(8,128)(2,1)}, u32[]{:S(2)}, u32[]{:S(2)}) collective-permute-start(bf16[128,4096]{1,0:T(8,128)(2,1)S(1)} %bitcast_select_fusion), channel_id=1, source_target_pairs={{1,0},{2,1},{3,2},{5,4},{6,5},{7,6},{9,8},{10,9},{11,10},{13,12},{... | collective-permute-start | bytes 3145736 | tf_op jit(solution)/shard_map/ppermute | solution.py:15
  21.3 68.6 %collective-permute-start.3 = (bf16[128,4096]{1,0:T(8,128)(2,1)S(1)}, bf16[128,4096]{1,0:T(8,128)(2,1)S(1)}, u32[]{:S(2)}, u32[]{:S(2)}) collective-permute-start(bf16[128,4096]{1,0:T(8,128)(2,1)S(1)} %bitcast_select_fusion), channel_id=1, source_target_pairs={{2,0},{3,1},{6,4},{7,5},{10,8},{11,9},{14,12},{15,13},{18,16},{19,... | collective-permute-start | bytes 3145736 | tf_op jit(solution)/shard_map/ppermute | solution.py:15
Sparse Core Ops, SparseCore 0:
  95.5 43.8 reduce-scatter.1
where the time goes:
time: 148 us
  waiting for transfers between devices  90.5 us (61%)
  matrix products  18.2 us (12%)
  between operations  14.2 us (10%)
  starting transfers between devices  14 us (9%)
  other arithmetic  9.55 us (6%)
  local copies, waits for them, and re-layouts  1.52 us (1%)
    ppermute x4, waiting for transfers between devices, passed_along(): return lax.ppermute(value, axis, pairs)  46.5 us
    reduce_scatter x1, waiting for transfers between devices, local(): lax.psum_scatter(jnp.stack(term_list), 'seg', scatter_dimension=1, tiled=...  44 us
    dot_general x4, matrix products, local(): jnp.dot(nearby, kernel, preferred_element_type=jnp.float32)  18.2 us
    ppermute x4, starting transfers between devices, passed_along(): return lax.ppermute(value, axis, pairs)  14 us
  transfers between devices with their start and end apart: 5, of which 4 were waited for; matrix products, arithmetic and copies ran while one was open for 14% of the time, Pallas kernels for 0%

commit v1 on v0

v1 whole, which is shorter than its diff:
```python
import functools
import math

import ml_dtypes
import numpy as np

import jax
import jax.numpy as jnp
from jax import lax
from jax.experimental import pallas as pl
from jax.experimental.pallas import tpu as pltpu
from jax.sharding import PartitionSpec as P

LAGS = 16
REACH = 2
GROUPS = 2
CHUNK = 512
MESH = pl.DeviceIdType.MESH


def make_table(bin_count, lag_count):
    lag_index = np.arange(lag_count)[:, None] - lag_count // 2
    turn_count = np.mod(np.arange(bin_count)[None, :] * lag_index, 2 * bin_count)
    phase_angle = turn_count.astype(np.float32) * np.float32(math.pi / bin_count)
    scaling = np.float32(1.0 / math.sqrt(2.0 * bin_count))
    both = np.stack([np.cos(phase_angle) * scaling, -np.sin(phase_angle) * scaling])
    return both.astype(ml_dtypes.bfloat16).astype(np.float32)


def body(n, nz, spectra, table, chosen, count, out, own, src, kbuf_a, kbuf_b, acc,
         part, landed, back, own_send, fwd_send, src_recv, part_send, part_recv,
         back_send, back_recv):
    k = lax.axis_index("seg")
    m = lax.axis_index("blk")
    channels, width = spectra.shape
    bins = width // 2
    rows = channels // n
    group = own.shape[1]
    cols = group * LAGS

    barrier = pltpu.get_barrier_semaphore()

    @pl.loop(1, n)
    def _(rel):
        pl.semaphore_signal(barrier, inc=1, device_id={"seg": lax.rem(k + rel, n)},
                            device_id_type=MESH)

    def along(dz):
        return jnp.logical_and(m + dz >= 0, m + dz < nz)

    for dz in (-2, -1, 1, 2):
        @pl.when(along(dz))
        def _():
            pl.semaphore_signal(barrier, inc=1, device_id={"blk": m + dz}, device_id_type=MESH)

    lane = lax.broadcasted_iota(jnp.int32, (GROUPS * group, channels), 1)
    hit = jnp.logical_and(lane == chosen[...], lane < count[0])
    one_hot = jnp.where(hit, 1.0, 0.0).astype(jnp.bfloat16)
    for c in range(width // CHUNK):
        at = pl.ds(c * CHUNK, CHUNK)
        picked = jnp.dot(one_hot, spectra[:, at], preferred_element_type=jnp.float32)
        picked = picked.astype(jnp.bfloat16)
        for g in range(GROUPS):
            own[g, :, at] = picked[g * group:(g + 1) * group]
    live = lax.broadcasted_iota(jnp.int32, (channels, 1), 0) < count[0]
    live = jnp.where(live, 1.0, 0.0)

    near = jnp.minimum(m, REACH) + jnp.minimum(nz - 1 - m, REACH)
    pl.semaphore_wait(barrier, n - 1 + near)

    def slot_of(side, dist):
        return 1 + dist if side == 0 else 2 - dist

    def step(side):
        return 1 if side == 0 else -1

    def own_copy(side, g):
        return pltpu.make_async_remote_copy(
            own.at[g], src.at[slot_of(side, 1), g], own_send.at[side, g],
            src_recv.at[slot_of(side, 1), g], device_id={"blk": m + step(side)},
            device_id_type=MESH)

    def fwd_copy(side, g):
        return pltpu.make_async_remote_copy(
            src.at[slot_of(side, 1), g], src.at[slot_of(side, 2), g], fwd_send.at[side, g],
            src_recv.at[slot_of(side, 2), g], device_id={"blk": m + step(side)},
            device_id_type=MESH)

    def part_copy(slot, g, peer, sender):
        return pltpu.make_async_remote_copy(
            part.at[slot, g, peer], landed.at[slot, g, sender], part_send.at[slot, g, peer],
            part_recv.at[slot, g, sender], device_id={"seg": peer}, device_id_type=MESH)

    def back_copy(slot, g, owner):
        at = pl.ds(pl.multiple_of(g * cols, cols), cols)
        return pltpu.make_async_remote_copy(
            back.at[slot, g], out.at[slot, :, at], back_send.at[slot, g],
            back_recv.at[slot, g], device_id={"blk": owner}, device_id_type=MESH)

    def has(side, dist):
        return m >= dist if side == 0 else m + dist < nz

    for g in range(GROUPS):
        for side in range(2):
            @pl.when(along(step(side)))
            def _():
                own_copy(side, g).start()

    def expand(slot, g, first, kbuf):
        re_at, im_at = pl.ds(first, CHUNK), pl.ds(bins + first, CHUNK)
        t_re, t_im = table[0, :, re_at], table[1, :, re_at]
        s_re = src[slot, g, :, re_at].astype(jnp.float32)
        s_im = src[slot, g, :, im_at].astype(jnp.float32)
        for j in range(group):
            a, b = s_re[j:j + 1], s_im[j:j + 1]
            to = slice(j * LAGS, (j + 1) * LAGS)
            kbuf[to, :CHUNK] = (a * t_re + b * t_im).astype(jnp.bfloat16)
            kbuf[to, CHUNK:] = (b * t_re - a * t_im).astype(jnp.bfloat16)

    def contract(first, kbuf):
        dims = (((1,), (1,)), ((), ()))
        got = lax.dot_general(kbuf[:, :CHUNK], spectra[:, pl.ds(first, CHUNK)], dims,
                              preferred_element_type=jnp.float32)
        return got + lax.dot_general(kbuf[:, CHUNK:], spectra[:, pl.ds(bins + first, CHUNK)],
                                     dims, preferred_element_type=jnp.float32)

    def correlate(slot, g):
        acc[...] = jnp.zeros_like(acc)

        @pl.loop(0, bins // (2 * CHUNK))
        def _(i):
            first = pl.multiple_of(i * 2 * CHUNK, CHUNK)
            second = pl.multiple_of(first + CHUNK, CHUNK)
            expand(slot, g, first, kbuf_a)
            got = contract(first, kbuf_a)
            expand(slot, g, second, kbuf_b)
            acc[...] += got + contract(second, kbuf_b)

        turned = acc[...].T * live
        for q in range(n):
            part[slot, g, q] = turned[q * rows:(q + 1) * rows].astype(jnp.bfloat16)

        @pl.loop(1, n)
        def _(rel):
            part_copy(slot, g, lax.rem(k + rel, n), k).start()

    def finish(p):
        dist, g = p // GROUPS + 1, p % GROUPS
        for side in range(2):
            slot = slot_of(side, dist)

            @pl.when(has(side, dist))
            def _():
                total = part[slot, g, k].astype(jnp.float32)
                for rel in range(1, n):
                    sender = lax.rem(k + rel, n)
                    part_copy(slot, g, sender, sender).wait_recv()
                    total = total + landed[slot, g, sender].astype(jnp.float32)
                back[slot, g] = total.astype(jnp.bfloat16)
                back_copy(slot, g, m - dist * step(side)).start()

    @pl.loop(0, REACH * GROUPS)
    def _(p):
        dist, g = p // GROUPS + 1, p % GROUPS
        for side in range(2):
            @pl.when(has(side, dist))
            def _():
                slot = slot_of(side, dist)
                pltpu.make_async_copy(src.at[slot, g], src.at[slot, g],
                                      src_recv.at[slot, g]).wait()

                @pl.when(jnp.logical_and(dist == 1, along(step(side))))
                def _():
                    fwd_copy(side, g).start()

        for side in range(2):
            @pl.when(has(side, dist))
            def _():
                correlate(slot_of(side, dist), g)

        @pl.when(p > 0)
        def _():
            finish(p - 1)

    finish(REACH * GROUPS - 1)

    for slot in range(2 * REACH):
        offset = slot - REACH if slot < REACH else slot - REACH + 1

        @pl.when(jnp.logical_not(along(offset)))
        def _():
            out[slot] = jnp.zeros(out.shape[1:], out.dtype)

        @pl.when(along(offset))
        def _():
            for g in range(GROUPS):
                back_copy(slot, g, m + offset).wait_recv()

    for g in range(GROUPS):
        for side in range(2):
            @pl.when(along(step(side)))
            def _():
                own_copy(side, g).wait_send()

            @pl.when(jnp.logical_and(has(side, 1), along(step(side))))
            def _():
                fwd_copy(side, g).wait_send()

            for dist in range(1, REACH + 1):
                @pl.when(has(side, dist))
                def _():
                    slot = slot_of(side, dist)
                    back_copy(slot, g, m - dist * step(side)).wait_send()

                    @pl.loop(1, n)
                    def _(rel):
                        part_copy(slot, g, lax.rem(k + rel, n), k).wait_send()


def local(n, nz, spectra, source_channels, pair_mask, channel_counts):
    own_block = spectra[0, 0]
    channels, width = own_block.shape
    sources = source_channels.shape[1]
    group = sources // GROUPS
    rows, cols, slots = channels // n, group * LAGS, 2 * REACH
    table = jnp.asarray(make_table(width // 2, LAGS))
    vmem = pl.BlockSpec(memory_space=pltpu.VMEM)
    dma = pltpu.SemaphoreType.DMA
    flops = 2 * slots * channels * width * sources * LAGS
    got = pl.pallas_call(
        functools.partial(body, n, nz),
        out_shape=jax.ShapeDtypeStruct((slots, rows, sources * LAGS), jnp.bfloat16),
        in_specs=[vmem, vmem, vmem, pl.BlockSpec(memory_space=pltpu.SMEM)],
        out_specs=vmem,
        scratch_shapes=[
            pltpu.VMEM((GROUPS, group, width), jnp.bfloat16),
            pltpu.VMEM((slots, GROUPS, group, width), jnp.bfloat16),
            pltpu.VMEM((cols, 2 * CHUNK), jnp.bfloat16),
            pltpu.VMEM((cols, 2 * CHUNK), jnp.bfloat16),
            pltpu.VMEM((cols, channels), jnp.float32),
            pltpu.VMEM((slots, GROUPS, n, rows, cols), jnp.bfloat16),
            pltpu.VMEM((slots, GROUPS, n, rows, cols), jnp.bfloat16),
            pltpu.VMEM((slots, GROUPS, rows, cols), jnp.bfloat16),
            dma((2, GROUPS)),
            dma((2, GROUPS)),
            dma((slots, GROUPS)),
            dma((slots, GROUPS, n)),
            dma((slots, GROUPS, n)),
            dma((slots, GROUPS)),
            dma((slots, GROUPS)),
        ],
        compiler_params=pltpu.CompilerParams(
            collective_id=0, has_side_effects=True, vmem_limit_bytes=40 * 2**20),
        cost_estimate=pl.CostEstimate(flops=flops, bytes_accessed=2 * channels * width,
                                      transcendentals=0),
    )(own_block, table, source_channels.reshape(sources, 1), channel_counts)
    weights = pair_mask[0].astype(jnp.float32) * (1.0 / math.sqrt(n))
    return (got.astype(jnp.float32) * weights[:, None, None])[None]


def solution(mesh):
    in_specs = (P("seg", "blk", None, None), P("blk", None), P("blk", None), P("blk"))
    out_specs = P("blk", None, "seg", None)
    part = functools.partial(local, mesh.shape["seg"], mesh.shape["blk"])
    return jax.shard_map(part, mesh=mesh, in_specs=in_specs, out_specs=out_specs, check_vma=False)
```

time: 148 us -> 45.1 us (0.30)
  waiting for transfers between devices: 90.5 us -> 0 us
  Pallas kernels: 0 us -> 39.9 us
  matrix products: 18.2 us -> 0 us
  starting transfers between devices: 14 us -> 0 us
  between operations: 14.2 us -> 0.67 us
  other arithmetic: 9.55 us -> 0.79 us
  local copies, waits for them, and re-layouts: 1.52 us -> 3.57 us
    ppermute x4 -> x0, waiting for transfers between devices: 46.5 us -> none  [passed_along(): return lax.ppermute(value, axis, pairs)]
    reduce_scatter x1 -> x0, waiting for transfers between devices: 44 us -> none  [local(): lax.psum_scatter(jnp.stack(term_list), 'seg', scatter_dimension=1, tiled=...]
    pallas_call x0 -> x1, Pallas kernels: none -> 39.9 us  [local(): pl.pallas_call(functools.partial(body, n, nz), out_shape=jax.ShapeDtypeSt...]
    dot_general x4 -> x0, matrix products: 18.2 us -> none  [local(): jnp.dot(nearby, kernel, preferred_element_type=jnp.float32)]
    ppermute x4 -> x0, starting transfers between devices: 14 us -> none  [passed_along(): return lax.ppermute(value, axis, pairs)]
    another operation x2 -> x0, other arithmetic: 4.35 us -> none
    unnamed x2 -> x8, local copies, waits for them, and re-layouts: 0.01 us -> 3.47 us
    select_n x3 -> x0, other arithmetic: 2.14 us -> none  [the longest x1 1.36 us: local(): own_block = jnp.where(live_rows, own_block, jnp.zeros_like(own_block))]
  transfers between devices with their start and end apart: 5 -> 0, of which waited for: 4 -> 0; matrix products, arithmetic and copies ran while one was open for 14% -> 0% of each run, Pallas kernels for 0% -> 0%
where the time goes in v1:
time: 45.1 us; the launch traced here: 44.9 us
  Pallas kernels  39.9 us (88%)
  local copies, waits for them, and re-layouts  3.57 us (8%)
  other arithmetic  0.79 us (2%)
  between operations  0.67 us (1%)
    pallas_call x1, Pallas kernels, local(): pl.pallas_call(functools.partial(body, n, nz), out_shape=jax.ShapeDtypeSt...  39.9 us
    unnamed x8, local copies, waits for them, and re-layouts  3.47 us

profile of v1, /device:TPU:0, one launch (start us, length us, event | category | flops | bytes accessed | tf_op | source)
XLA Modules:
  0.0 44.9 jit_solution(11170107902593467810)
XLA Ops:
  0.7 0.0 copy-start.3
  0.7 0.6 %copy-done.3 = s32[1,4]{1,0:T(1,128)S(1)} copy-done((s32[1,4]{1,0:T(1,128)S(1)}, s32[1,4]{1,0:T(1,128)}, u32[]{:S(2)}) %copy-start.3) | copy-done | bytes 40
  1.3 0.0 copy-start.2
  1.3 0.6 %copy-done.2 = s32[1,64]{1,0:T(1,128)S(1)} copy-done((s32[1,64]{1,0:T(1,128)S(1)}, s32[1,64]{1,0:T(1,128)}, u32[]{:S(2)}) %copy-start.2) | copy-done | bytes 280
  2.0 0.1 copy.6.chosen
  2.1 0.0 copy-start
  2.1 1.2 %copy-done = bf16[1,1,128,4096]{3,2,1,0:T(8,128)(2,1)S(1)} copy-done((bf16[1,1,128,4096]{3,2,1,0:T(8,128)(2,1)S(1)}, bf16[1,1,128,4096]{3,2,1,0:T(8,128)(2,1)}, u32[]{:S(2)}) %copy-start) | copy-done | bytes 1048600
  3.3 0.0 copy-start.1
  3.3 0.9 %copy-done.1 = f32[2,16,2048]{2,1,0:T(8,128)S(1)} copy-done((f32[2,16,2048]{2,1,0:T(8,128)S(1)}, f32[2,16,2048]{2,1,0:T(8,128)}, u32[]{:S(2)}) %copy-start.1) | copy-done | bytes 262168
  4.2 39.9 %shard_map.55 = bf16[4,16,1024]{2,1,0:T(8,128)(2,1)S(1)} custom-call(bf16[128,4096]{1,0:T(8,128)(2,1)S(1)} %bitcast.6, f32[2,16,2048]{2,1,0:T(8,128)S(1)} %copy-done.1, s32[64,1]{1,0:T(8,128)S(1)} %copy.6.chosen, s32[1]{0:T(128)S(6)} %copy.7.count), custom_call_target="tpu_custom_call" | custom-call | flops 4294967296 | bytes 1048576 | tf_op jit(solution)/shard_map/pallas_call | solution.py:230
  44.1 0.8 %multiply_bitcast_fusion = f32[1,4,16,1024]{3,2,1,0:T(8,128)} fusion(bf16[4,16,1024]{2,1,0:T(8,128)(2,1)S(1)} %shard_map.55, f32[4]{0:T(128)S(1)} %multiply_bitcast_fusion.1), kind=kLoop, calls=%fused_computation | loop fusion | flops 131072 | bytes 393232 | tf_op jit(solution)/shard_map/broadcast_in_dim | solution.py:258
  (1 shorter events, 0.0 us)
Async XLA Ops:
  0.7 0.7 %copy-start.3 = (s32[1,4]{1,0:T(1,128)S(1)}, s32[1,4]{1,0:T(1,128)}, u32[]{:S(2)}) copy-start(s32[1,4]{1,0:T(1,128)} %param.7) | copy-start | bytes 52
  1.3 0.7 %copy-start.2 = (s32[1,64]{1,0:T(1,128)S(1)}, s32[1,64]{1,0:T(1,128)}, u32[]{:S(2)}) copy-start(s32[1,64]{1,0:T(1,128)} %param.6) | copy-start | bytes 772
  2.1 1.2 %copy-start = (bf16[1,1,128,4096]{3,2,1,0:T(8,128)(2,1)S(1)}, bf16[1,1,128,4096]{3,2,1,0:T(8,128)(2,1)}, u32[]{:S(2)}) copy-start(bf16[1,1,128,4096]{3,2,1,0:T(8,128)(2,1)} %param.5) | copy-start | bytes 3145732
  3.3 0.9 %copy-start.1 = (f32[2,16,2048]{2,1,0:T(8,128)S(1)}, f32[2,16,2048]{2,1,0:T(8,128)}, u32[]{:S(2)}) copy-start(f32[2,16,2048]{2,1,0:T(8,128)} %constant.4.clone.table) | copy-start | bytes 786436

commit v2 on v1

v2 whole, which is shorter than its diff:
```python
import functools
import math

import ml_dtypes
import numpy as np

import jax
import jax.numpy as jnp
from jax import lax
from jax.experimental import pallas as pl
from jax.experimental.pallas import tpu as pltpu
from jax.sharding import PartitionSpec as P

LAGS = 16
REACH = 2
GROUPS = 2
PIECES = 4
PICK = 512
MESH = pl.DeviceIdType.MESH


def make_table(bin_count, lag_count):
    lag_index = np.arange(lag_count)[:, None] - lag_count // 2
    turn_count = np.mod(np.arange(bin_count)[None, :] * lag_index, 2 * bin_count)
    phase_angle = turn_count.astype(np.float32) * np.float32(math.pi / bin_count)
    scaling = np.float32(1.0 / math.sqrt(2.0 * bin_count))
    both = np.stack([np.cos(phase_angle) * scaling, -np.sin(phase_angle) * scaling])
    return both.astype(ml_dtypes.bfloat16)


def body(n, nz, spectra_in, table_in, chosen_in, count_in, out, spectra, table, chosen, count,
         own, src, kbuf_a, kbuf_b, acc, part, landed, back, in_sem, own_send, fwd_send, src_recv,
         part_send, part_recv, back_send, back_recv):
    arrivals = [
        pltpu.make_async_copy(here, there, in_sem.at[i])
        for i, (here, there) in enumerate([(chosen_in, chosen), (count_in, count),
                                           (spectra_in, spectra), (table_in, table)])
    ]
    for arrival in arrivals:
        arrival.start()

    k = lax.axis_index("seg")
    m = lax.axis_index("blk")
    channels, width = spectra.shape
    bins = width // 2
    rows = channels // n
    group = own.shape[2]
    cols = group * LAGS
    span = bins // PIECES
    chunk = span // 2

    barrier = pltpu.get_barrier_semaphore()

    @pl.loop(1, n)
    def _(rel):
        pl.semaphore_signal(barrier, inc=1, device_id={"seg": lax.rem(k + rel, n)},
                            device_id_type=MESH)

    def along(dz):
        return jnp.logical_and(m + dz >= 0, m + dz < nz)

    for dz in (-2, -1, 1, 2):
        @pl.when(along(dz))
        def _():
            pl.semaphore_signal(barrier, inc=1, device_id={"blk": m + dz}, device_id_type=MESH)

    for arrival in arrivals:
        arrival.wait()

    channel = lax.broadcasted_iota(jnp.int32, (channels, GROUPS * group), 0)
    hit = jnp.logical_and(channel == chosen[...], channel < count[0])
    one_hot = jnp.where(hit, 1.0, 0.0).T.astype(jnp.bfloat16)
    for i in range(PIECES):
        for half in range(2):
            for c in range(0, span, PICK):
                picked = jnp.dot(one_hot, spectra[:, pl.ds(half * bins + i * span + c, PICK)],
                                 preferred_element_type=jnp.float32).astype(jnp.bfloat16)
                for g in range(GROUPS):
                    own[g, i, :, pl.ds(half * span + c, PICK)] = picked[g * group:(g + 1) * group]
    live = lax.broadcasted_iota(jnp.int32, (channels, 1), 0) < count[0]
    live = jnp.where(live, 1.0, 0.0)

    near = jnp.minimum(m, REACH) + jnp.minimum(nz - 1 - m, REACH)
    pl.semaphore_wait(barrier, n - 1 + near)

    def slot_of(side, dist):
        return 1 + dist if side == 0 else 2 - dist

    def step(side):
        return 1 if side == 0 else -1

    def own_copy(side, g, i):
        return pltpu.make_async_remote_copy(
            own.at[g, i], src.at[slot_of(side, 1), g, i], own_send.at[side, g, i],
            src_recv.at[slot_of(side, 1), g, i], device_id={"blk": m + step(side)},
            device_id_type=MESH)

    def fwd_copy(side, g, i):
        return pltpu.make_async_remote_copy(
            src.at[slot_of(side, 1), g, i], src.at[slot_of(side, 2), g, i],
            fwd_send.at[side, g, i], src_recv.at[slot_of(side, 2), g, i],
            device_id={"blk": m + step(side)}, device_id_type=MESH)

    def src_wait(slot, g, i):
        here = src.at[slot, g, i]
        pltpu.make_async_copy(here, here, src_recv.at[slot, g, i]).wait()

    def part_copy(slot, g, peer, sender):
        return pltpu.make_async_remote_copy(
            part.at[slot, g, peer], landed.at[slot, g, sender], part_send.at[slot, g, peer],
            part_recv.at[slot, g, sender], device_id={"seg": peer}, device_id_type=MESH)

    def back_copy(slot, g, owner):
        at = pl.ds(pl.multiple_of(g * cols, cols), cols)
        return pltpu.make_async_remote_copy(
            back.at[slot, g], out.at[slot, :, at], back_send.at[slot, g],
            back_recv.at[slot, g], device_id={"blk": owner}, device_id_type=MESH)

    def has(side, dist):
        return m >= dist if side == 0 else m + dist < nz

    for g in range(GROUPS):
        for side in range(2):
            @pl.when(along(step(side)))
            def _():
                for i in range(PIECES):
                    own_copy(side, g, i).start()

    def expand(slot, g, i, part_of, kbuf):
        at = pl.ds(pl.multiple_of(i * span + part_of * chunk, chunk), chunk)
        t_re, t_im = table[0, :, at], table[1, :, at]
        s_re = src[slot, g, i, :, pl.ds(part_of * chunk, chunk)]
        s_im = src[slot, g, i, :, pl.ds(span + part_of * chunk, chunk)]
        for j in range(group):
            a, b = s_re[j:j + 1], s_im[j:j + 1]
            to = slice(j * LAGS, (j + 1) * LAGS)
            kbuf[to, :chunk] = a * t_re + b * t_im
            kbuf[to, chunk:] = b * t_re - a * t_im

    def contract(i, part_of, kbuf):
        dims = (((1,), (1,)), ((), ()))
        first = pl.multiple_of(i * span + part_of * chunk, chunk)
        got = lax.dot_general(kbuf[:, :chunk], spectra[:, pl.ds(first, chunk)], dims,
                              preferred_element_type=jnp.float32)
        return got + lax.dot_general(kbuf[:, chunk:], spectra[:, pl.ds(bins + first, chunk)],
                                     dims, preferred_element_type=jnp.float32)

    def correlate(slot, dist, g):
        acc[...] = jnp.zeros_like(acc)

        @pl.loop(0, PIECES)
        def _(i):
            @pl.when(dist > 1)
            def _():
                src_wait(slot, g, i)

            expand(slot, g, i, 0, kbuf_a)
            got = contract(i, 0, kbuf_a)
            expand(slot, g, i, 1, kbuf_b)
            acc[...] += got + contract(i, 1, kbuf_b)

        turned = acc[...].T * live
        for q in range(n):
            part[slot, g, q] = turned[q * rows:(q + 1) * rows].astype(jnp.bfloat16)

        @pl.loop(1, n)
        def _(rel):
            part_copy(slot, g, lax.rem(k + rel, n), k).start()

    def finish(p):
        dist, g = p // GROUPS + 1, p % GROUPS
        for side in range(2):
            slot = slot_of(side, dist)

            @pl.when(has(side, dist))
            def _():
                total = part[slot, g, k].astype(jnp.float32)
                for rel in range(1, n):
                    sender = lax.rem(k + rel, n)
                    part_copy(slot, g, sender, sender).wait_recv()
                    total = total + landed[slot, g, sender].astype(jnp.float32)
                back[slot, g] = total.astype(jnp.bfloat16)
                back_copy(slot, g, m - dist * step(side)).start()

    @pl.loop(0, REACH * GROUPS)
    def _(p):
        dist, g = p // GROUPS + 1, p % GROUPS
        for side in range(2):
            for i in range(PIECES):
                @pl.when(jnp.logical_and(dist == 1, has(side, 1)))
                def _():
                    src_wait(slot_of(side, 1), g, i)

                    @pl.when(along(step(side)))
                    def _():
                        fwd_copy(side, g, i).start()

        for side in range(2):
            @pl.when(has(side, dist))
            def _():
                correlate(slot_of(side, dist), dist, g)

        @pl.when(p > 0)
        def _():
            finish(p - 1)

    finish(REACH * GROUPS - 1)

    for slot in range(2 * REACH):
        offset = slot - REACH if slot < REACH else slot - REACH + 1

        @pl.when(jnp.logical_not(along(offset)))
        def _():
            out[slot] = jnp.zeros(out.shape[1:], out.dtype)

        @pl.when(along(offset))
        def _():
            for g in range(GROUPS):
                back_copy(slot, g, m + offset).wait_recv()

    for g in range(GROUPS):
        for side in range(2):
            @pl.when(along(step(side)))
            def _():
                for i in range(PIECES):
                    own_copy(side, g, i).wait_send()

            @pl.when(jnp.logical_and(has(side, 1), along(step(side))))
            def _():
                for i in range(PIECES):
                    fwd_copy(side, g, i).wait_send()

            for dist in range(1, REACH + 1):
                @pl.when(has(side, dist))
                def _():
                    slot = slot_of(side, dist)
                    back_copy(slot, g, m - dist * step(side)).wait_send()

                    @pl.loop(1, n)
                    def _(rel):
                        part_copy(slot, g, lax.rem(k + rel, n), k).wait_send()


def local(n, nz, spectra, source_channels, pair_mask, channel_counts):
    own_block = spectra[0, 0]
    channels, width = own_block.shape
    sources = source_channels.shape[1]
    group = sources // GROUPS
    rows, cols, slots = channels // n, group * LAGS, 2 * REACH
    table = jnp.asarray(make_table(width // 2, LAGS))
    vmem = pl.BlockSpec(memory_space=pltpu.VMEM)
    dma = pltpu.SemaphoreType.DMA
    flops = 2 * slots * channels * width * sources * LAGS
    got = pl.pallas_call(
        functools.partial(body, n, nz),
        out_shape=jax.ShapeDtypeStruct((slots, rows, sources * LAGS), jnp.bfloat16),
        in_specs=[pl.BlockSpec(memory_space=pl.ANY)] * 4,
        out_specs=vmem,
        scratch_shapes=[
            pltpu.VMEM(own_block.shape, jnp.bfloat16),
            pltpu.VMEM(table.shape, jnp.bfloat16),
            pltpu.VMEM((1, sources), jnp.int32),
            pltpu.SMEM((1,), jnp.int32),
            pltpu.VMEM((GROUPS, PIECES, group, width // PIECES), jnp.bfloat16),
            pltpu.VMEM((slots, GROUPS, PIECES, group, width // PIECES), jnp.bfloat16),
            pltpu.VMEM((cols, width // PIECES // 2), jnp.bfloat16),
            pltpu.VMEM((cols, width // PIECES // 2), jnp.bfloat16),
            pltpu.VMEM((cols, channels), jnp.float32),
            pltpu.VMEM((slots, GROUPS, n, rows, cols), jnp.bfloat16),
            pltpu.VMEM((slots, GROUPS, n, rows, cols), jnp.bfloat16),
            pltpu.VMEM((slots, GROUPS, rows, cols), jnp.bfloat16),
            dma((4,)),
            dma((2, GROUPS, PIECES)),
            dma((2, GROUPS, PIECES)),
            dma((slots, GROUPS, PIECES)),
            dma((slots, GROUPS, n)),
            dma((slots, GROUPS, n)),
            dma((slots, GROUPS)),
            dma((slots, GROUPS)),
        ],
        compiler_params=pltpu.CompilerParams(
            collective_id=0, has_side_effects=True, vmem_limit_bytes=60 * 2**20),
        cost_estimate=pl.CostEstimate(flops=flops, bytes_accessed=2 * channels * width,
                                      transcendentals=0),
    )(own_block, table, source_channels, channel_counts)
    weights = pair_mask[0].astype(jnp.float32) * (1.0 / math.sqrt(n))
    return (got.astype(jnp.float32) * weights[:, None, None])[None]


def solution(mesh):
    in_specs = (P("seg", "blk", None, None), P("blk", None), P("blk", None), P("blk"))
    out_specs = P("blk", None, "seg", None)
    part = functools.partial(local, mesh.shape["seg"], mesh.shape["blk"])
    return jax.shard_map(part, mesh=mesh, in_specs=in_specs, out_specs=out_specs, check_vma=False)
```

time: 45.1 us -> 42.9 us (0.951)
  local copies, waits for them, and re-layouts: 3.57 us -> 0.65 us
  other arithmetic: 0.79 us -> 1.7 us
    unnamed x8 -> x2, local copies, waits for them, and re-layouts: 3.47 us -> 0.65 us
    broadcast_in_dim x1, other arithmetic: 0.79 us -> 1.69 us  [local(): return (got.astype(jnp.float32) * weights[:, None, None])[None]]
where the time goes in v2:
time: 42.9 us; the launch traced here: 42.8 us
  Pallas kernels  39.8 us (93%)
  other arithmetic  1.7 us (4%)
  between operations  0.67 us (2%)
  local copies, waits for them, and re-layouts  0.65 us (2%)
    pallas_call x1, Pallas kernels, local(): pl.pallas_call(functools.partial(body, n, nz), out_shape=jax.ShapeDtypeSt...  39.8 us
    broadcast_in_dim x1, other arithmetic, local(): return (got.astype(jnp.float32) * weights[:, None, None])[None]  1.69 us

profile of v2, /device:TPU:0, one launch (start us, length us, event | category | flops | bytes accessed | tf_op | source)
XLA Modules:
  0.0 42.8 jit_solution(6601187342016844845)
XLA Ops:
  0.7 0.0 copy-start
  0.7 0.6 %copy-done = s32[1,4]{1,0:T(1,128)S(1)} copy-done((s32[1,4]{1,0:T(1,128)S(1)}, s32[1,4]{1,0:T(1,128)}, u32[]{:S(2)}) %copy-start) | copy-done | bytes 40
  1.3 39.8 %shard_map.55 = bf16[4,16,1024]{2,1,0:T(8,128)(2,1)} custom-call(bf16[128,4096]{1,0:T(8,128)(2,1)} %bitcast.5, bf16[2,16,2048]{2,1,0:T(8,128)(2,1)} %constant.4.clone.table_in, s32[1,64]{1,0:T(1,128)} %chosen_in.1, s32[1]{0:T(128)S(6)} %copy.6.count_in), custom_call_target="tpu_custom_call" | custom-call | flops 4294967296 | bytes 1048576 | tf_op jit(solution)/shard_map/pallas_call | solution.py:254
  41.1 1.7 %multiply_bitcast_fusion = f32[1,4,16,1024]{3,2,1,0:T(8,128)} fusion(bf16[4,16,1024]{2,1,0:T(8,128)(2,1)} %shard_map.55, f32[4]{0:T(128)S(1)} %multiply_bitcast_fusion.1), kind=kLoop, calls=%fused_computation | loop fusion | flops 131072 | bytes 393232 | tf_op jit(solution)/shard_map/broadcast_in_dim | solution.py:287
  (1 shorter events, 0.0 us)
Async XLA Ops:
  0.7 0.7 %copy-start = (s32[1,4]{1,0:T(1,128)S(1)}, s32[1,4]{1,0:T(1,128)}, u32[]{:S(2)}) copy-start(s32[1,4]{1,0:T(1,128)} %param.7) | copy-start | bytes 52

commit v3 on v2

--- a/solution.py
+++ b/solution.py
@@ -15,6 +15,7 @@
 REACH = 2
 GROUPS = 2
 PIECES = 4
+AHEAD = 4
 PICK = 512
 MESH = pl.DeviceIdType.MESH
 
@@ -28,13 +29,13 @@
     return both.astype(ml_dtypes.bfloat16)
 
 
-def body(n, nz, spectra_in, table_in, chosen_in, count_in, out, spectra, table, chosen, count,
+def body(n, nz, spectra_in, table_in, chosen_in, count, out, spectra, table, chosen,
          own, src, kbuf_a, kbuf_b, acc, part, landed, back, in_sem, own_send, fwd_send, src_recv,
          part_send, part_recv, back_send, back_recv):
     arrivals = [
         pltpu.make_async_copy(here, there, in_sem.at[i])
-        for i, (here, there) in enumerate([(chosen_in, chosen), (count_in, count),
-                                           (spectra_in, spectra), (table_in, table)])
+        for i, (here, there) in enumerate(
+            [(chosen_in, chosen), (spectra_in, spectra), (table_in, table)])
     ]
     for arrival in arrivals:
         arrival.start()
@@ -70,13 +71,16 @@
     channel = lax.broadcasted_iota(jnp.int32, (channels, GROUPS * group), 0)
     hit = jnp.logical_and(channel == chosen[...], channel < count[0])
     one_hot = jnp.where(hit, 1.0, 0.0).T.astype(jnp.bfloat16)
-    for i in range(PIECES):
+
+    def pick(i):
         for half in range(2):
             for c in range(0, span, PICK):
                 picked = jnp.dot(one_hot, spectra[:, pl.ds(half * bins + i * span + c, PICK)],
                                  preferred_element_type=jnp.float32).astype(jnp.bfloat16)
                 for g in range(GROUPS):
                     own[g, i, :, pl.ds(half * span + c, PICK)] = picked[g * group:(g + 1) * group]
+
+    pick(0)
     live = lax.broadcasted_iota(jnp.int32, (channels, 1), 0) < count[0]
     live = jnp.where(live, 1.0, 0.0)
 
@@ -119,12 +123,26 @@
     def has(side, dist):
         return m >= dist if side == 0 else m + dist < nz
 
-    for g in range(GROUPS):
-        for side in range(2):
-            @pl.when(along(step(side)))
-            def _():
-                for i in range(PIECES):
-                    own_copy(side, g, i).start()
+    near_steps = GROUPS * PIECES
+    all_steps = REACH * near_steps
+
+    def send(t):
+        g, i = lax.rem(t // PIECES, GROUPS), lax.rem(t, PIECES)
+        for side in range(2):
+            @pl.when(jnp.logical_and(t < near_steps, along(step(side))))
+            def _():
+                own_copy(side, g, i).start()
+
+            relay = jnp.logical_and(t >= near_steps, t < all_steps)
+
+            @pl.when(jnp.logical_and(relay, jnp.logical_and(has(side, 1), along(step(side)))))
+            def _():
+                fwd_copy(side, g, i).start()
+
+    for t in range(AHEAD):
+        send(jnp.int32(t))
+        if t + 1 < PIECES:
+            pick(t + 1)
 
     def expand(slot, g, i, part_of, kbuf):
         at = pl.ds(pl.multiple_of(i * span + part_of * chunk, chunk), chunk)
@@ -145,21 +163,22 @@
         return got + lax.dot_general(kbuf[:, chunk:], spectra[:, pl.ds(bins + first, chunk)],
                                      dims, preferred_element_type=jnp.float32)
 
-    def correlate(slot, dist, g):
-        acc[...] = jnp.zeros_like(acc)
-
-        @pl.loop(0, PIECES)
-        def _(i):
-            @pl.when(dist > 1)
-            def _():
-                src_wait(slot, g, i)
-
-            expand(slot, g, i, 0, kbuf_a)
-            got = contract(i, 0, kbuf_a)
-            expand(slot, g, i, 1, kbuf_b)
-            acc[...] += got + contract(i, 1, kbuf_b)
-
-        turned = acc[...].T * live
+    def correlate(side, slot, g, i):
+        expand(slot, g, i, 0, kbuf_a)
+        got = contract(i, 0, kbuf_a)
+        expand(slot, g, i, 1, kbuf_b)
+        got = got + contract(i, 1, kbuf_b)
+
+        @pl.when(i == 0)
+        def _():
+            acc[side] = got
+
+        @pl.when(i > 0)
+        def _():
+            acc[side] += got
+
+    def share(side, slot, g):
+        turned = acc[side].T * live
         for q in range(n):
             part[slot, g, q] = turned[q * rows:(q + 1) * rows].astype(jnp.bfloat16)
 
@@ -182,25 +201,27 @@
                 back[slot, g] = total.astype(jnp.bfloat16)
                 back_copy(slot, g, m - dist * step(side)).start()
 
-    @pl.loop(0, REACH * GROUPS)
-    def _(p):
-        dist, g = p // GROUPS + 1, p % GROUPS
-        for side in range(2):
-            for i in range(PIECES):
-                @pl.when(jnp.logical_and(dist == 1, has(side, 1)))
+    @pl.loop(0, all_steps)
+    def _(t):
+        p, i = t // PIECES, lax.rem(t, PIECES)
+        dist, g = p // GROUPS + 1, lax.rem(p, GROUPS)
+        for side in range(2):
+            @pl.when(has(side, dist))
+            def _():
+                src_wait(slot_of(side, dist), g, i)
+
+        send(t + AHEAD)
+        for side in range(2):
+            @pl.when(has(side, dist))
+            def _():
+                slot = slot_of(side, dist)
+                correlate(side, slot, g, i)
+
+                @pl.when(i == PIECES - 1)
                 def _():
-                    src_wait(slot_of(side, 1), g, i)
-
-                    @pl.when(along(step(side)))
-                    def _():
-                        fwd_copy(side, g, i).start()
-
-        for side in range(2):
-            @pl.when(has(side, dist))
-            def _():
-                correlate(slot_of(side, dist), dist, g)
-
-        @pl.when(p > 0)
+                    share(side, slot, g)
+
+        @pl.when(jnp.logical_and(i == PIECES // 2, p > 0))
         def _():
             finish(p - 1)
 
@@ -254,22 +275,21 @@
     got = pl.pallas_call(
         functools.partial(body, n, nz),
         out_shape=jax.ShapeDtypeStruct((slots, rows, sources * LAGS), jnp.bfloat16),
-        in_specs=[pl.BlockSpec(memory_space=pl.ANY)] * 4,
+        in_specs=[pl.BlockSpec(memory_space=pltpu.HBM)] * 3 + [pl.BlockSpec(memory_space=pltpu.SMEM)],
         out_specs=vmem,
         scratch_shapes=[
             pltpu.VMEM(own_block.shape, jnp.bfloat16),
             pltpu.VMEM(table.shape, jnp.bfloat16),
             pltpu.VMEM((1, sources), jnp.int32),
-            pltpu.SMEM((1,), jnp.int32),
             pltpu.VMEM((GROUPS, PIECES, group, width // PIECES), jnp.bfloat16),
             pltpu.VMEM((slots, GROUPS, PIECES, group, width // PIECES), jnp.bfloat16),
             pltpu.VMEM((cols, width // PIECES // 2), jnp.bfloat16),
             pltpu.VMEM((cols, width // PIECES // 2), jnp.bfloat16),
-            pltpu.VMEM((cols, channels), jnp.float32),
+            pltpu.VMEM((2, cols, channels), jnp.float32),
             pltpu.VMEM((slots, GROUPS, n, rows, cols), jnp.bfloat16),
             pltpu.VMEM((slots, GROUPS, n, rows, cols), jnp.bfloat16),
             pltpu.VMEM((slots, GROUPS, rows, cols), jnp.bfloat16),
-            dma((4,)),
+            dma((3,)),
             dma((2, GROUPS, PIECES)),
             dma((2, GROUPS, PIECES)),
             dma((slots, GROUPS, PIECES)),
@@ -279,7 +299,7 @@
             dma((slots, GROUPS)),
         ],
         compiler_params=pltpu.CompilerParams(
-            collective_id=0, has_side_effects=True, vmem_limit_bytes=60 * 2**20),
+            collective_id=0, has_side_effects=True, vmem_limit_bytes=40 * 2**20),
         cost_estimate=pl.CostEstimate(flops=flops, bytes_accessed=2 * channels * width,
                                       transcendentals=0),
     )(own_block, table, source_channels, channel_counts)

time: 42.9 us -> 45 us (1.049)
  local copies, waits for them, and re-layouts: 0.65 us -> 3.43 us
  other arithmetic: 1.7 us -> 0.79 us
    unnamed x2 -> x8, local copies, waits for them, and re-layouts: 0.65 us -> 3.43 us
    broadcast_in_dim x1, other arithmetic: 1.69 us -> 0.79 us  [local(): return (got.astype(jnp.float32) * weights[:, None, None])[None]]
where the time goes in v3:
time: 45 us; the launch traced here: 44.8 us
  Pallas kernels  39.9 us (89%)
  local copies, waits for them, and re-layouts  3.43 us (8%)
  other arithmetic  0.79 us (2%)
  between operations  0.67 us (1%)
    pallas_call x1, Pallas kernels, local(): pl.pallas_call(functools.partial(body, n, nz), out_shape=jax.ShapeDtypeSt...  39.9 us
    unnamed x8, local copies, waits for them, and re-layouts  3.43 us

profile of v3, /device:TPU:0, one launch (start us, length us, event | category | flops | bytes accessed | tf_op | source)
XLA Modules:
  0.0 44.8 jit_solution(12811088728430626656)
XLA Ops:
  0.7 0.0 copy-start.3
  0.7 0.6 %copy-done.3 = s32[1,4]{1,0:T(1,128)S(1)} copy-done((s32[1,4]{1,0:T(1,128)S(1)}, s32[1,4]{1,0:T(1,128)}, u32[]{:S(2)}) %copy-start.3) | copy-done | bytes 40
  1.3 0.0 copy-start.1
  1.3 0.6 %copy-done.1 = s32[1,64]{1,0:T(1,128)S(1)} copy-done((s32[1,64]{1,0:T(1,128)S(1)}, s32[1,64]{1,0:T(1,128)}, u32[]{:S(2)}) %copy-start.1) | copy-done | bytes 280
  2.0 0.0 copy-start
  2.0 1.2 %copy-done = bf16[1,1,128,4096]{3,2,1,0:T(8,128)(2,1)S(1)} copy-done((bf16[1,1,128,4096]{3,2,1,0:T(8,128)(2,1)S(1)}, bf16[1,1,128,4096]{3,2,1,0:T(8,128)(2,1)}, u32[]{:S(2)}) %copy-start) | copy-done | bytes 1048600
  3.2 0.0 copy-start.2
  3.2 0.9 %copy-done.2 = bf16[2,16,2048]{2,1,0:T(8,128)(2,1)S(1)} copy-done((bf16[2,16,2048]{2,1,0:T(8,128)(2,1)S(1)}, bf16[2,16,2048]{2,1,0:T(8,128)(2,1)}, u32[]{:S(2)}) %copy-start.2) | copy-done | bytes 131096
  4.1 39.9 %shard_map.55 = bf16[4,16,1024]{2,1,0:T(8,128)(2,1)S(1)} custom-call(bf16[128,4096]{1,0:T(8,128)(2,1)S(1)} %bitcast.5, bf16[2,16,2048]{2,1,0:T(8,128)(2,1)S(1)} %copy-done.2, s32[1,64]{1,0:T(1,128)S(1)} %copy-done.1, s32[1]{0:T(128)S(6)} %copy.6.count), custom_call_target="tpu_custom_call" | custom-call | flops 4294967296 | bytes 1048576 | tf_op jit(solution)/shard_map/pallas_call | solution.py:275
  44.0 0.8 %multiply_bitcast_fusion = f32[1,4,16,1024]{3,2,1,0:T(8,128)} fusion(bf16[4,16,1024]{2,1,0:T(8,128)(2,1)S(1)} %shard_map.55, f32[4]{0:T(128)S(1)} %multiply_bitcast_fusion.1), kind=kLoop, calls=%fused_computation | loop fusion | flops 131072 | bytes 393232 | tf_op jit(solution)/shard_map/broadcast_in_dim | solution.py:307
  (1 shorter events, 0.0 us)
Async XLA Ops:
  0.7 0.7 %copy-start.3 = (s32[1,4]{1,0:T(1,128)S(1)}, s32[1,4]{1,0:T(1,128)}, u32[]{:S(2)}) copy-start(s32[1,4]{1,0:T(1,128)} %param.7) | copy-start | bytes 52
  1.3 0.7 %copy-start.1 = (s32[1,64]{1,0:T(1,128)S(1)}, s32[1,64]{1,0:T(1,128)}, u32[]{:S(2)}) copy-start(s32[1,64]{1,0:T(1,128)} %chosen_in.1) | copy-start | bytes 772
  2.0 1.2 %copy-start = (bf16[1,1,128,4096]{3,2,1,0:T(8,128)(2,1)S(1)}, bf16[1,1,128,4096]{3,2,1,0:T(8,128)(2,1)}, u32[]{:S(2)}) copy-start(bf16[1,1,128,4096]{3,2,1,0:T(8,128)(2,1)} %param.5) | copy-start | bytes 3145732
  3.2 0.9 %copy-start.2 = (bf16[2,16,2048]{2,1,0:T(8,128)(2,1)S(1)}, bf16[2,16,2048]{2,1,0:T(8,128)(2,1)}, u32[]{:S(2)}) copy-start(bf16[2,16,2048]{2,1,0:T(8,128)(2,1)} %constant.4.clone.table_in) | copy-start | bytes 393220

commit v4 on v3

--- a/solution.py
+++ b/solution.py
@@ -15,8 +15,8 @@
 REACH = 2
 GROUPS = 2
 PIECES = 4
-AHEAD = 4
-PICK = 512
+AHEAD = 6
+PICK = 256
 MESH = pl.DeviceIdType.MESH
 
 
@@ -30,7 +30,7 @@
 
 
 def body(n, nz, spectra_in, table_in, chosen_in, count, out, spectra, table, chosen,
-         own, src, kbuf_a, kbuf_b, acc, part, landed, back, in_sem, own_send, fwd_send, src_recv,
+         own, src, turned, wide, kbuf, acc, part, landed, back, in_sem, own_send, fwd_send, src_recv,
          part_send, part_recv, back_send, back_recv):
     arrivals = [
         pltpu.make_async_copy(here, there, in_sem.at[i])
@@ -48,7 +48,7 @@
     group = own.shape[2]
     cols = group * LAGS
     span = bins // PIECES
-    chunk = span // 2
+    half_cols = cols // 2
 
     barrier = pltpu.get_barrier_semaphore()
 
@@ -144,43 +144,37 @@
         if t + 1 < PIECES:
             pick(t + 1)
 
-    def expand(slot, g, i, part_of, kbuf):
-        at = pl.ds(pl.multiple_of(i * span + part_of * chunk, chunk), chunk)
-        t_re, t_im = table[0, :, at], table[1, :, at]
-        s_re = src[slot, g, i, :, pl.ds(part_of * chunk, chunk)]
-        s_im = src[slot, g, i, :, pl.ds(span + part_of * chunk, chunk)]
-        for j in range(group):
-            a, b = s_re[j:j + 1], s_im[j:j + 1]
-            to = slice(j * LAGS, (j + 1) * LAGS)
-            kbuf[to, :chunk] = a * t_re + b * t_im
-            kbuf[to, chunk:] = b * t_re - a * t_im
-
-    def contract(i, part_of, kbuf):
-        dims = (((1,), (1,)), ((), ()))
-        first = pl.multiple_of(i * span + part_of * chunk, chunk)
-        got = lax.dot_general(kbuf[:, :chunk], spectra[:, pl.ds(first, chunk)], dims,
-                              preferred_element_type=jnp.float32)
-        return got + lax.dot_general(kbuf[:, chunk:], spectra[:, pl.ds(bins + first, chunk)],
-                                     dims, preferred_element_type=jnp.float32)
+    for i in range(PIECES):
+        for half in range(2):
+            for c in range(0, span, PICK):
+                block = spectra[:, pl.ds(half * bins + i * span + c, PICK)]
+                turned[i, pl.ds(half * span + c, PICK), :] = block.T
+
+    acc[...] = jnp.zeros_like(acc)
 
     def correlate(side, slot, g, i):
-        expand(slot, g, i, 0, kbuf_a)
-        got = contract(i, 0, kbuf_a)
-        expand(slot, g, i, 1, kbuf_b)
-        got = got + contract(i, 1, kbuf_b)
-
-        @pl.when(i == 0)
-        def _():
-            acc[side] = got
-
-        @pl.when(i > 0)
-        def _():
-            acc[side] += got
+        wide[...] = src[slot, g, i].astype(jnp.float32)
+        for h in range(2):
+            for c in range(0, span, PICK):
+                t_re = table[0, :, pl.ds(pl.multiple_of(i * span + c, PICK), PICK)]
+                t_im = table[1, :, pl.ds(pl.multiple_of(i * span + c, PICK), PICK)]
+                for j in range(group // 2):
+                    row = h * (group // 2) + j
+                    a = jnp.broadcast_to(wide[row:row + 1, c:c + PICK], (LAGS, PICK))
+                    b = jnp.broadcast_to(wide[row:row + 1, span + c:span + c + PICK],
+                                         (LAGS, PICK))
+                    a, b = a.astype(jnp.bfloat16), b.astype(jnp.bfloat16)
+                    to = slice(j * LAGS, (j + 1) * LAGS)
+                    kbuf[h, to, c:c + PICK] = a * t_re + b * t_im
+                    kbuf[h, to, span + c:span + c + PICK] = b * t_re - a * t_im
+            acc[side, h * half_cols:(h + 1) * half_cols] += jnp.dot(
+                kbuf[h], turned[i], preferred_element_type=jnp.float32)
 
     def share(side, slot, g):
-        turned = acc[side].T * live
+        result = acc[side].T * live
+        acc[side] = jnp.zeros(acc.shape[1:], acc.dtype)
         for q in range(n):
-            part[slot, g, q] = turned[q * rows:(q + 1) * rows].astype(jnp.bfloat16)
+            part[slot, g, q] = result[q * rows:(q + 1) * rows].astype(jnp.bfloat16)
 
         @pl.loop(1, n)
         def _(rel):
@@ -275,7 +269,7 @@
     got = pl.pallas_call(
         functools.partial(body, n, nz),
         out_shape=jax.ShapeDtypeStruct((slots, rows, sources * LAGS), jnp.bfloat16),
-        in_specs=[pl.BlockSpec(memory_space=pltpu.HBM)] * 3 + [pl.BlockSpec(memory_space=pltpu.SMEM)],
+        in_specs=[pl.BlockSpec(memory_space=pl.ANY)] * 3 + [pl.BlockSpec(memory_space=pltpu.SMEM)],
         out_specs=vmem,
         scratch_shapes=[
             pltpu.VMEM(own_block.shape, jnp.bfloat16),
@@ -283,8 +277,9 @@
             pltpu.VMEM((1, sources), jnp.int32),
             pltpu.VMEM((GROUPS, PIECES, group, width // PIECES), jnp.bfloat16),
             pltpu.VMEM((slots, GROUPS, PIECES, group, width // PIECES), jnp.bfloat16),
-            pltpu.VMEM((cols, width // PIECES // 2), jnp.bfloat16),
-            pltpu.VMEM((cols, width // PIECES // 2), jnp.bfloat16),
+            pltpu.VMEM((PIECES, width // PIECES, channels), jnp.bfloat16),
+            pltpu.VMEM((group, width // PIECES), jnp.float32),
+            pltpu.VMEM((2, cols // 2, width // PIECES), jnp.bfloat16),
             pltpu.VMEM((2, cols, channels), jnp.float32),
             pltpu.VMEM((slots, GROUPS, n, rows, cols), jnp.bfloat16),
             pltpu.VMEM((slots, GROUPS, n, rows, cols), jnp.bfloat16),
@@ -299,7 +294,7 @@
             dma((slots, GROUPS)),
         ],
         compiler_params=pltpu.CompilerParams(
-            collective_id=0, has_side_effects=True, vmem_limit_bytes=40 * 2**20),
+            collective_id=0, has_side_effects=True, vmem_limit_bytes=60 * 2**20),
         cost_estimate=pl.CostEstimate(flops=flops, bytes_accessed=2 * channels * width,
                                       transcendentals=0),
     )(own_block, table, source_channels, channel_counts)

time: 45 us -> 43.2 us (0.960)
  local copies, waits for them, and re-layouts: 3.43 us -> 0.65 us
  other arithmetic: 0.79 us -> 1.7 us
    unnamed x8 -> x2, local copies, waits for them, and re-layouts: 3.43 us -> 0.65 us
    broadcast_in_dim x1, other arithmetic: 0.79 us -> 1.69 us  [local(): return (got.astype(jnp.float32) * weights[:, None, None])[None]]
where the time goes in v4:
time: 43.2 us; the launch traced here: 43.1 us
  Pallas kernels  40 us (93%)
  other arithmetic  1.7 us (4%)
  between operations  0.67 us (2%)
  local copies, waits for them, and re-layouts  0.65 us (2%)
    pallas_call x1, Pallas kernels, local(): pl.pallas_call(functools.partial(body, n, nz), out_shape=jax.ShapeDtypeSt...  40 us
    broadcast_in_dim x1, other arithmetic, local(): return (got.astype(jnp.float32) * weights[:, None, None])[None]  1.69 us

profile of v4, /device:TPU:0, one launch (start us, length us, event | category | flops | bytes accessed | tf_op | source)
XLA Modules:
  0.0 43.1 jit_solution(16110702031509360048)
XLA Ops:
  0.7 0.0 copy-start
  0.7 0.6 %copy-done = s32[1,4]{1,0:T(1,128)S(1)} copy-done((s32[1,4]{1,0:T(1,128)S(1)}, s32[1,4]{1,0:T(1,128)}, u32[]{:S(2)}) %copy-start) | copy-done | bytes 40
  1.3 40.0 %shard_map.55 = bf16[4,16,1024]{2,1,0:T(8,128)(2,1)} custom-call(bf16[128,4096]{1,0:T(8,128)(2,1)} %bitcast.5, bf16[2,16,2048]{2,1,0:T(8,128)(2,1)} %constant.4.clone.table_in, s32[1,64]{1,0:T(1,128)} %chosen_in.1, s32[1]{0:T(128)S(6)} %copy.6.count), custom_call_target="tpu_custom_call" | custom-call | flops 4294967296 | bytes 1048576 | tf_op jit(solution)/shard_map/pallas_call | solution.py:269
  41.4 1.7 %multiply_bitcast_fusion = f32[1,4,16,1024]{3,2,1,0:T(8,128)} fusion(bf16[4,16,1024]{2,1,0:T(8,128)(2,1)} %shard_map.55, f32[4]{0:T(128)S(1)} %multiply_bitcast_fusion.1), kind=kLoop, calls=%fused_computation | loop fusion | flops 131072 | bytes 393232 | tf_op jit(solution)/shard_map/broadcast_in_dim | solution.py:302
  (1 shorter events, 0.0 us)
Async XLA Ops:
  0.7 0.7 %copy-start = (s32[1,4]{1,0:T(1,128)S(1)}, s32[1,4]{1,0:T(1,128)}, u32[]{:S(2)}) copy-start(s32[1,4]{1,0:T(1,128)} %param.7) | copy-start | bytes 52

commit v5 on v4

--- a/solution.py
+++ b/solution.py
@@ -13,8 +13,8 @@
 
 LAGS = 16
 REACH = 2
-GROUPS = 2
-PIECES = 4
+GROUPS = 4
+PIECES = 2
 AHEAD = 6
 PICK = 256
 MESH = pl.DeviceIdType.MESH
@@ -29,13 +29,15 @@
     return both.astype(ml_dtypes.bfloat16)
 
 
-def body(n, nz, spectra_in, table_in, chosen_in, count, out, spectra, table, chosen,
+def body(n, nz, spectra_in, table_in, chosen_in, count_in, pairs_in, out, spectra, table, chosen,
+         count, pairs, home,
          own, src, turned, wide, kbuf, acc, part, landed, back, in_sem, own_send, fwd_send, src_recv,
          part_send, part_recv, back_send, back_recv):
     arrivals = [
         pltpu.make_async_copy(here, there, in_sem.at[i])
         for i, (here, there) in enumerate(
-            [(chosen_in, chosen), (spectra_in, spectra), (table_in, table)])
+            [(chosen_in, chosen), (count_in, count), (spectra_in, spectra), (pairs_in, pairs),
+             (table_in, table)])
     ]
     for arrival in arrivals:
         arrival.start()
@@ -69,7 +71,7 @@
         arrival.wait()
 
     channel = lax.broadcasted_iota(jnp.int32, (channels, GROUPS * group), 0)
-    hit = jnp.logical_and(channel == chosen[...], channel < count[0])
+    hit = jnp.logical_and(channel == chosen[...], channel < count[...])
     one_hot = jnp.where(hit, 1.0, 0.0).T.astype(jnp.bfloat16)
 
     def pick(i):
@@ -81,7 +83,7 @@
                     own[g, i, :, pl.ds(half * span + c, PICK)] = picked[g * group:(g + 1) * group]
 
     pick(0)
-    live = lax.broadcasted_iota(jnp.int32, (channels, 1), 0) < count[0]
+    live = lax.broadcasted_iota(jnp.int32, (channels, 1), 0) < count[...]
     live = jnp.where(live, 1.0, 0.0)
 
     near = jnp.minimum(m, REACH) + jnp.minimum(nz - 1 - m, REACH)
@@ -117,7 +119,7 @@
     def back_copy(slot, g, owner):
         at = pl.ds(pl.multiple_of(g * cols, cols), cols)
         return pltpu.make_async_remote_copy(
-            back.at[slot, g], out.at[slot, :, at], back_send.at[slot, g],
+            back.at[slot, g], home.at[slot, :, at], back_send.at[slot, g],
             back_recv.at[slot, g], device_id={"blk": owner}, device_id_type=MESH)
 
     def has(side, dist):
@@ -232,6 +234,8 @@
         def _():
             for g in range(GROUPS):
                 back_copy(slot, g, m + offset).wait_recv()
+            weight = pairs[:, slot:slot + 1].astype(jnp.float32) * (1.0 / math.sqrt(n))
+            out[slot] = home[slot].astype(jnp.float32) * weight
 
     for g in range(GROUPS):
         for side in range(2):
@@ -268,13 +272,16 @@
     flops = 2 * slots * channels * width * sources * LAGS
     got = pl.pallas_call(
         functools.partial(body, n, nz),
-        out_shape=jax.ShapeDtypeStruct((slots, rows, sources * LAGS), jnp.bfloat16),
-        in_specs=[pl.BlockSpec(memory_space=pl.ANY)] * 3 + [pl.BlockSpec(memory_space=pltpu.SMEM)],
+        out_shape=jax.ShapeDtypeStruct((slots, rows, sources * LAGS), jnp.float32),
+        in_specs=[pl.BlockSpec(memory_space=pl.ANY)] * 5,
         out_specs=vmem,
         scratch_shapes=[
             pltpu.VMEM(own_block.shape, jnp.bfloat16),
             pltpu.VMEM(table.shape, jnp.bfloat16),
             pltpu.VMEM((1, sources), jnp.int32),
+            pltpu.VMEM((1, 1), jnp.int32),
+            pltpu.VMEM((1, slots), jnp.int32),
+            pltpu.VMEM((slots, rows, sources * LAGS), jnp.bfloat16),
             pltpu.VMEM((GROUPS, PIECES, group, width // PIECES), jnp.bfloat16),
             pltpu.VMEM((slots, GROUPS, PIECES, group, width // PIECES), jnp.bfloat16),
             pltpu.VMEM((PIECES, width // PIECES, channels), jnp.bfloat16),
@@ -284,7 +291,7 @@
             pltpu.VMEM((slots, GROUPS, n, rows, cols), jnp.bfloat16),
             pltpu.VMEM((slots, GROUPS, n, rows, cols), jnp.bfloat16),
             pltpu.VMEM((slots, GROUPS, rows, cols), jnp.bfloat16),
-            dma((3,)),
+            dma((5,)),
             dma((2, GROUPS, PIECES)),
             dma((2, GROUPS, PIECES)),
             dma((slots, GROUPS, PIECES)),
@@ -297,9 +304,8 @@
             collective_id=0, has_side_effects=True, vmem_limit_bytes=60 * 2**20),
         cost_estimate=pl.CostEstimate(flops=flops, bytes_accessed=2 * channels * width,
                                       transcendentals=0),
-    )(own_block, table, source_channels, channel_counts)
-    weights = pair_mask[0].astype(jnp.float32) * (1.0 / math.sqrt(n))
-    return (got.astype(jnp.float32) * weights[:, None, None])[None]
+    )(own_block, table, source_channels, channel_counts.reshape(1, 1), pair_mask)
+    return got[None]
 
 
 def solution(mesh):

time: 43.2 us -> 44.6 us (1.032)
  Pallas kernels: 40 us -> 42.1 us
  other arithmetic: 1.7 us -> 0 us
  local copies, waits for them, and re-layouts: 0.65 us -> 1.67 us
    pallas_call x1, Pallas kernels: 40 us -> 42.1 us  [local(): pl.pallas_call(functools.partial(body, n, nz), out_shape=jax.ShapeDtypeSt...]
    broadcast_in_dim x1 -> x0, other arithmetic: 1.69 us -> none  [local(): return (got.astype(jnp.float32) * weights[:, None, None])[None]]
    unnamed x2 -> x1, local copies, waits for them, and re-layouts: 0.65 us -> 1.67 us
where the time goes in v5:
time: 44.6 us; the launch traced here: 44.4 us
  Pallas kernels  42.1 us (94%)
  local copies, waits for them, and re-layouts  1.67 us (4%)
  between operations  0.66 us (1%)
    pallas_call x1, Pallas kernels, local(): pl.pallas_call(functools.partial(body, n, nz), out_shape=jax.ShapeDtypeSt...  42.1 us
    unnamed x1, local copies, waits for them, and re-layouts  1.67 us

profile of v5, /device:TPU:0, one launch (start us, length us, event | category | flops | bytes accessed | tf_op | source)
XLA Modules:
  0.0 44.4 jit_solution(17737458071901496680)
XLA Ops:
  0.7 42.1 %shard_map.55 = f32[4,16,1024]{2,1,0:T(8,128)} custom-call(bf16[128,4096]{1,0:T(8,128)(2,1)} %bitcast.5, bf16[2,16,2048]{2,1,0:T(8,128)(2,1)} %constant.2.clone.table_in, s32[1,64]{1,0:T(1,128)} %chosen_in.1, s32[1,1]{1,0:T(1,128)} %bitcast.3.count_in, s32[1,4]{1,0:T(1,128)} %pairs_in.1), custom_call_target="tpu_custom_call" | custom-call | flops 4294967296 | bytes 1048576 | tf_op jit(solution)/shard_map/pallas_call | solution.py:273
  42.7 1.7 %copy.8 = f32[1,4,16,1024]{3,2,1,0:T(8,128)} copy(f32[1,4,16,1024]{3,2,1,0:T(8,128)} %bitcast.4) | data formatting | bytes 524288

commit v6 on v2

--- a/solution.py
+++ b/solution.py
@@ -279,7 +279,7 @@
             dma((slots, GROUPS)),
         ],
         compiler_params=pltpu.CompilerParams(
-            collective_id=0, has_side_effects=True, vmem_limit_bytes=60 * 2**20),
+            collective_id=0, has_side_effects=True, vmem_limit_bytes=53 * 2**20),
         cost_estimate=pl.CostEstimate(flops=flops, bytes_accessed=2 * channels * width,
                                       transcendentals=0),
     )(own_block, table, source_channels, channel_counts)

time: 42.9 us -> 43.3 us (level)
  local copies, waits for them, and re-layouts: 0.65 us -> 2.2 us
  other arithmetic: 1.7 us -> 0.79 us
    unnamed x2 -> x6, local copies, waits for them, and re-layouts: 0.65 us -> 2.2 us
    broadcast_in_dim x1, other arithmetic: 1.69 us -> 0.79 us  [local(): return (got.astype(jnp.float32) * weights[:, None, None])[None]]
where the time goes in v6:
time: 43.3 us; the launch traced here: 43.1 us
  Pallas kernels  39.5 us (91%)
  local copies, waits for them, and re-layouts  2.2 us (5%)
  other arithmetic  0.79 us (2%)
  between operations  0.67 us (2%)
    pallas_call x1, Pallas kernels, local(): pl.pallas_call(functools.partial(body, n, nz), out_shape=jax.ShapeDtypeSt...  39.5 us
    unnamed x6, local copies, waits for them, and re-layouts  2.2 us

profile of v6, /device:TPU:0, one launch (start us, length us, event | category | flops | bytes accessed | tf_op | source)
XLA Modules:
  0.0 43.1 jit_solution(6141032400882659590)
XLA Ops:
  0.7 0.0 copy-start.2
  0.7 0.6 %copy-done.2 = s32[1,4]{1,0:T(1,128)S(1)} copy-done((s32[1,4]{1,0:T(1,128)S(1)}, s32[1,4]{1,0:T(1,128)}, u32[]{:S(2)}) %copy-start.2) | copy-done | bytes 40
  1.3 0.0 copy-start
  1.3 0.6 %copy-done = s32[1,64]{1,0:T(1,128)S(1)} copy-done((s32[1,64]{1,0:T(1,128)S(1)}, s32[1,64]{1,0:T(1,128)}, u32[]{:S(2)}) %copy-start) | copy-done | bytes 280
  2.0 0.0 copy-start.1
  2.0 0.9 %copy-done.1 = bf16[2,16,2048]{2,1,0:T(8,128)(2,1)S(1)} copy-done((bf16[2,16,2048]{2,1,0:T(8,128)(2,1)S(1)}, bf16[2,16,2048]{2,1,0:T(8,128)(2,1)}, u32[]{:S(2)}) %copy-start.1) | copy-done | bytes 131096
  2.9 39.5 %shard_map.55 = bf16[4,16,1024]{2,1,0:T(8,128)(2,1)S(1)} custom-call(bf16[128,4096]{1,0:T(8,128)(2,1)} %bitcast.5, bf16[2,16,2048]{2,1,0:T(8,128)(2,1)S(1)} %copy-done.1, s32[1,64]{1,0:T(1,128)S(1)} %copy-done, s32[1]{0:T(128)S(6)} %copy.6.count_in), custom_call_target="tpu_custom_call" | custom-call | flops 4294967296 | bytes 1048576 | tf_op jit(solution)/shard_map/pallas_call | solution.py:254
  42.3 0.8 %multiply_bitcast_fusion = f32[1,4,16,1024]{3,2,1,0:T(8,128)} fusion(bf16[4,16,1024]{2,1,0:T(8,128)(2,1)S(1)} %shard_map.55, f32[4]{0:T(128)S(1)} %multiply_bitcast_fusion.1), kind=kLoop, calls=%fused_computation | loop fusion | flops 131072 | bytes 393232 | tf_op jit(solution)/shard_map/broadcast_in_dim | solution.py:287
  (1 shorter events, 0.0 us)
Async XLA Ops:
  0.7 0.7 %copy-start.2 = (s32[1,4]{1,0:T(1,128)S(1)}, s32[1,4]{1,0:T(1,128)}, u32[]{:S(2)}) copy-start(s32[1,4]{1,0:T(1,128)} %param.7) | copy-start | bytes 52
  1.3 0.7 %copy-start = (s32[1,64]{1,0:T(1,128)S(1)}, s32[1,64]{1,0:T(1,128)}, u32[]{:S(2)}) copy-start(s32[1,64]{1,0:T(1,128)} %chosen_in.1) | copy-start | bytes 772
  2.0 0.9 %copy-start.1 = (bf16[2,16,2048]{2,1,0:T(8,128)(2,1)S(1)}, bf16[2,16,2048]{2,1,0:T(8,128)(2,1)}, u32[]{:S(2)}) copy-start(bf16[2,16,2048]{2,1,0:T(8,128)(2,1)} %constant.4.clone.table_in) | copy-start | bytes 393220
